TPU v7x, 32 devices: a whole 2x2x4 slice. The times are simulated.
32 devices in a mesh: dp: 8 (over z, y), fsdp: 4 (over x, core).
Axes of the slice: x: 2, y: 2, z: 4, core: 2. Of those that a mesh axis runs over, the one named last changes fastest.
Arguments:
- patches: bfloat16 [16384, 768], P(('dp', 'fsdp')), may hold values from -6 to 6
- order: int32 [128, 196], P(('dp', 'fsdp')), may hold values from 0 to 195, each once within a row
- grad_latent: float32 [16384, 768], P(('dp', 'fsdp')), may hold values from -6 to 6
- grad_out: float32 [16384, 768], P(('dp', 'fsdp')), may hold values from -6 to 6
- pos_embed: bfloat16 [196, 768], P(None, ('dp', 'fsdp')), may hold values from -6 to 6
- ln_gain: bfloat16 [2, 2, 768], P(None, None, ('dp', 'fsdp')), may hold values from 0.099609375 to 1.8984375
- ln_bias: bfloat16 [2, 2, 768], P(None, None, ('dp', 'fsdp')), may hold values from -2 to 2
- w_qkv: bfloat16 [2, 768, 2304], P(None, ('dp', 'fsdp')), may hold values from -0.21875 to 0.21875
- b_qkv: bfloat16 [2, 1536], P(None, ('dp', 'fsdp')), may hold values from -2 to 2
- w_proj: bfloat16 [2, 768, 768], P(None, ('dp', 'fsdp')), may hold values from -0.875 to 0.875
- b_proj: bfloat16 [2, 768], P(None, ('dp', 'fsdp')), may hold values from -2 to 2
- w_fc1: bfloat16 [2, 768, 3072], P(None, ('dp', 'fsdp')), may hold values from -0.21875 to 0.21875
- b_fc1: bfloat16 [2, 3072], P(None, ('dp', 'fsdp')), may hold values from -2 to 2
- w_fc2: bfloat16 [2, 3072, 768], P(None, ('dp', 'fsdp')), may hold values from -0.15625 to 0.15625
- b_fc2: bfloat16 [2, 768], P(None, ('dp', 'fsdp')), may hold values from -2 to 2
- layer_scale: bfloat16 [2, 2, 768], P(None, None, ('dp', 'fsdp')), may hold values from 0.5 to 1.5
Outputs:
- latent: bfloat16 [16384, 768], P(('dp', 'fsdp'))
- regressed: bfloat16 [16384, 768], P(('dp', 'fsdp'))
- grad_patches: float32 [16384, 768], P(('dp', 'fsdp'))
- grad_pos: float32 [196, 768], P(None, ('dp', 'fsdp'))
- grad_ln_gain: float32 [2, 2, 768], P(None, None, ('dp', 'fsdp'))
- grad_ln_bias: float32 [2, 2, 768], P(None, None, ('dp', 'fsdp'))
- grad_w_qkv: float32 [2, 768, 2304], P(None, ('dp', 'fsdp'))
- grad_b_qkv: float32 [2, 1536], P(None, ('dp', 'fsdp'))
- grad_w_proj: float32 [2, 768, 768], P(None, ('dp', 'fsdp'))
- grad_b_proj: float32 [2, 768], P(None, ('dp', 'fsdp'))
- grad_w_fc1: float32 [2, 768, 3072], P(None, ('dp', 'fsdp'))
- grad_b_fc1: float32 [2, 3072], P(None, ('dp', 'fsdp'))
- grad_w_fc2: float32 [2, 3072, 768], P(None, ('dp', 'fsdp'))
- grad_b_fc2: float32 [2, 768], P(None, ('dp', 'fsdp'))
- grad_layer_scale: float32 [2, 2, 768], P(None, None, ('dp', 'fsdp'))
Inputs may be any that keep to these rules, and one draw needn't show every extreme that they name: Each row of order holds every patch number of the image once; its first 98 entries are the visible patches and the rest the masked ones.
All inputs are finite; a program needn't handle non-finite values.
Results may differ from a plain program's by a relative error of at most 0.013.
Values may be sent and summed in bfloat16 or wider, within the bound.
A program may use at most 256 MiB of HBM per device.

v0:
```python
import functools
import math

import jax
import jax.numpy as jnp
from jax import lax
from jax.sharding import PartitionSpec as P

HEAD_DIM = 64
VIS = 98
SET = 128
PATCHES = 196


def norm_forward(value, gain, shift):
    center = jnp.mean(value, axis=-1, keepdims=True)
    centered = value - center
    inverse = lax.rsqrt(jnp.mean(centered * centered, axis=-1, keepdims=True) + 1e-06)
    normed = centered * inverse
    return (normed * gain + shift, normed, inverse)


def norm_backward(grad, normed, inverse, gain):
    scaled = grad * gain
    first_mean = jnp.mean(scaled, axis=-1, keepdims=True)
    second_mean = jnp.mean(scaled * normed, axis=-1, keepdims=True)
    back = inverse * (scaled - first_mean - normed * second_mean)
    return (back, jnp.sum(grad * normed, axis=0), jnp.sum(grad, axis=0))


def unpack(pieces):
    gains, shifts, w_qkv, b_qkv, w_proj, b_proj, w_fc1, b_fc1, w_fc2, b_fc2, scales = pieces
    wide = jnp.float32
    return (
        gains.astype(wide),
        shifts.astype(wide),
        w_qkv,
        b_qkv.astype(wide),
        w_proj,
        b_proj.astype(wide),
        w_fc1,
        b_fc1.astype(wide),
        w_fc2,
        b_fc2.astype(wide),
        scales.astype(wide),
    )


def fetch(block, arrays):
    ln_gain, ln_bias, w_qkv, b_qkv, w_proj, b_proj, w_fc1, b_fc1, w_fc2, b_fc2, layer_scale = arrays
    gathered = (
        lax.all_gather(ln_gain[block], ("dp", "fsdp"), axis=1, tiled=True),
        lax.all_gather(ln_bias[block], ("dp", "fsdp"), axis=1, tiled=True),
        lax.all_gather(w_qkv[block], ("dp", "fsdp"), axis=0, tiled=True),
        lax.all_gather(b_qkv[block], ("dp", "fsdp"), axis=0, tiled=True),
        lax.all_gather(w_proj[block], ("dp", "fsdp"), axis=0, tiled=True),
        lax.all_gather(b_proj[block], ("dp", "fsdp"), axis=0, tiled=True),
        lax.all_gather(w_fc1[block], ("dp", "fsdp"), axis=0, tiled=True),
        lax.all_gather(b_fc1[block], ("dp", "fsdp"), axis=0, tiled=True),
        lax.all_gather(w_fc2[block], ("dp", "fsdp"), axis=0, tiled=True),
        lax.all_gather(b_fc2[block], ("dp", "fsdp"), axis=0, tiled=True),
        lax.all_gather(layer_scale[block], ("dp", "fsdp"), axis=1, tiled=True),
    )
    return unpack(gathered)


def column_sum(value):
    return jnp.sum(value.astype(jnp.float32), axis=0)


def outer_rows(left, right):
    return jnp.einsum("rd,rf->df", left, right, preferred_element_type=jnp.float32)


def attend_scores(queries, keys, key_live):
    scores = jnp.einsum("gqhe,gkhe->ghqk", queries, keys, preferred_element_type=jnp.float32) * (
        1.0 / math.sqrt(HEAD_DIM)
    )
    return jnp.where(key_live, scores, -1e30)


def attend_forward(query_in, key_in, images, key_live, weights):
    w_qkv, b_qkv, w_proj, b_proj = (weights[2], weights[3], weights[4], weights[5])
    model = query_in.shape[1]
    heads = model // HEAD_DIM
    queries = (
        jnp.dot(query_in, w_qkv[:, :model], preferred_element_type=jnp.float32) + b_qkv[:model]
    ).astype(jnp.bfloat16)
    paired = jnp.dot(key_in, w_qkv[:, model:], preferred_element_type=jnp.float32)
    keys = paired[:, :model].astype(jnp.bfloat16).reshape(images, -1, heads, HEAD_DIM)
    values = (
        (paired[:, model:] + b_qkv[model:])
        .astype(jnp.bfloat16)
        .reshape(images, -1, heads, HEAD_DIM)
    )
    queries = queries.reshape(images, -1, heads, HEAD_DIM)
    scores = attend_scores(queries, keys, key_live)
    highest_score = jnp.max(scores, axis=-1, keepdims=True)
    weighted = jnp.exp(scores - highest_score)
    summed = jnp.sum(weighted, axis=-1, keepdims=True)
    softmax_out = (weighted / summed).astype(jnp.bfloat16)
    mixed = jnp.einsum("ghqk,gkhe->gqhe", softmax_out, values, preferred_element_type=jnp.float32)
    mixed = mixed.reshape(-1, model).astype(jnp.bfloat16)
    branch = jnp.dot(mixed, w_proj, preferred_element_type=jnp.float32) + b_proj
    return (branch, (queries, keys, values, highest_score + jnp.log(summed), mixed))


def attend_backward(grad_branch, query_in, key_in, key_live, kept, weights):
    w_qkv, w_proj = (weights[2], weights[4])
    queries, keys, values, log_total, mixed = kept
    model = query_in.shape[1]
    grad_low = grad_branch.astype(jnp.bfloat16)
    grad_w_proj = outer_rows(mixed, grad_low)
    grad_b_proj = column_sum(grad_low)
    grad_mixed = (
        jnp.dot(grad_low, w_proj.T, preferred_element_type=jnp.float32)
        .astype(jnp.bfloat16)
        .reshape(queries.shape)
    )
    softmax_out = jnp.exp(attend_scores(queries, keys, key_live) - log_total)
    grad_values = jnp.einsum(
        "ghqk,gqhe->gkhe",
        softmax_out.astype(jnp.bfloat16),
        grad_mixed,
        preferred_element_type=jnp.float32,
    )
    grad_soft = jnp.einsum(
        "gqhe,gkhe->ghqk", grad_mixed, values, preferred_element_type=jnp.float32
    )
    grad_scores = (
        softmax_out * (grad_soft - jnp.sum(grad_soft * softmax_out, axis=-1, keepdims=True))
    ).astype(jnp.bfloat16)
    factor = 1.0 / math.sqrt(HEAD_DIM)
    grad_queries = (
        (
            jnp.einsum("ghqk,gkhe->gqhe", grad_scores, keys, preferred_element_type=jnp.float32)
            * factor
        )
        .astype(jnp.bfloat16)
        .reshape(-1, model)
    )
    grad_keys = (
        (
            jnp.einsum("ghqk,gqhe->gkhe", grad_scores, queries, preferred_element_type=jnp.float32)
            * factor
        )
        .astype(jnp.bfloat16)
        .reshape(-1, model)
    )
    grad_values = grad_values.astype(jnp.bfloat16).reshape(-1, model)
    grad_pairs = jnp.concatenate([grad_keys, grad_values], axis=1)
    grad_w_qkv = jnp.concatenate(
        [outer_rows(query_in, grad_queries), outer_rows(key_in, grad_pairs)], axis=1
    )
    grad_b_qkv = jnp.concatenate([column_sum(grad_queries), column_sum(grad_values)])
    grad_query_in = jnp.dot(grad_queries, w_qkv[:, :model].T, preferred_element_type=jnp.float32)
    grad_key_in = jnp.dot(grad_pairs, w_qkv[:, model:].T, preferred_element_type=jnp.float32)
    return (grad_query_in, grad_key_in, (grad_w_qkv, grad_b_qkv, grad_w_proj, grad_b_proj))


def feed_forward(middle, weights):
    gains, shifts, w_fc1, b_fc1, w_fc2, b_fc2 = (
        weights[0],
        weights[1],
        weights[6],
        weights[7],
        weights[8],
        weights[9],
    )
    normed_out, normed, inverse = norm_forward(middle, gains[1], shifts[1])
    inner_in = normed_out.astype(jnp.bfloat16)
    hidden = jnp.dot(inner_in, w_fc1, preferred_element_type=jnp.float32) + b_fc1
    active = jax.nn.gelu(hidden, approximate=True).astype(jnp.bfloat16)
    branch = jnp.dot(active, w_fc2, preferred_element_type=jnp.float32) + b_fc2
    return (branch, (normed, inverse, inner_in, hidden, active))


def feed_backward(grad_branch, kept, weights):
    gains, w_fc1, w_fc2 = (weights[0], weights[6], weights[8])
    normed, inverse, inner_in, hidden, active = kept
    grad_low = grad_branch.astype(jnp.bfloat16)
    grad_w_fc2 = outer_rows(active, grad_low)
    grad_b_fc2 = column_sum(grad_low)
    grad_active = jnp.dot(grad_low, w_fc2.T, preferred_element_type=jnp.float32)
    gelu_back = jax.vjp(functools.partial(jax.nn.gelu, approximate=True), hidden)[1]
    grad_hidden = gelu_back(grad_active)[0].astype(jnp.bfloat16)
    grad_w_fc1 = outer_rows(inner_in, grad_hidden)
    grad_b_fc1 = column_sum(grad_hidden)
    grad_normed = jnp.dot(grad_hidden, w_fc1.T, preferred_element_type=jnp.float32)
    grad_middle, grad_gain, grad_shift = norm_backward(grad_normed, normed, inverse, gains[1])
    return (grad_middle, grad_gain, grad_shift, (grad_w_fc1, grad_b_fc1, grad_w_fc2, grad_b_fc2))


def local(
    patches,
    order,
    grad_latent,
    grad_out,
    pos_embed,
    ln_gain,
    ln_bias,
    w_qkv,
    b_qkv,
    w_proj,
    b_proj,
    w_fc1,
    b_fc1,
    w_fc2,
    b_fc2,
    layer_scale,
):
    arrays = (
        ln_gain,
        ln_bias,
        w_qkv,
        b_qkv,
        w_proj,
        b_proj,
        w_fc1,
        b_fc1,
        w_fc2,
        b_fc2,
        layer_scale,
    )
    images = order.shape[0]
    model = patches.shape[1]
    highest = lax.Precision.HIGHEST
    live = jnp.arange(SET) < VIS
    live_rows = jnp.tile(live, images).astype(jnp.float32)[:, None]
    patch_slots = jnp.arange(PATCHES)

    def picker(index):
        padded = jnp.pad(index, ((0, 0), (0, SET - VIS)))
        chosen = (padded[:, :, None] == patch_slots[None, None, :]) & live[None, :, None]
        return chosen.astype(jnp.float32).reshape(-1, PATCHES)

    pick_visible = picker(order[:, :VIS])
    pick_masked = picker(order[:, VIS:])
    gathered = (
        lax.all_gather(pos_embed, ("dp", "fsdp"), axis=1, tiled=True),
        lax.all_gather(ln_gain[0], ("dp", "fsdp"), axis=1, tiled=True),
        lax.all_gather(ln_bias[0], ("dp", "fsdp"), axis=1, tiled=True),
        lax.all_gather(w_qkv[0], ("dp", "fsdp"), axis=0, tiled=True),
        lax.all_gather(b_qkv[0], ("dp", "fsdp"), axis=0, tiled=True),
        lax.all_gather(w_proj[0], ("dp", "fsdp"), axis=0, tiled=True),
        lax.all_gather(b_proj[0], ("dp", "fsdp"), axis=0, tiled=True),
        lax.all_gather(w_fc1[0], ("dp", "fsdp"), axis=0, tiled=True),
        lax.all_gather(b_fc1[0], ("dp", "fsdp"), axis=0, tiled=True),
        lax.all_gather(w_fc2[0], ("dp", "fsdp"), axis=0, tiled=True),
        lax.all_gather(b_fc2[0], ("dp", "fsdp"), axis=0, tiled=True),
        lax.all_gather(layer_scale[0], ("dp", "fsdp"), axis=1, tiled=True),
    )
    pos_table = gathered[0].astype(jnp.float32)
    enc_weights = unpack(gathered[1:])
    start = patches.astype(jnp.float32) + jnp.dot(pick_visible, pos_table, precision=highest)
    enc_out, enc_normed, enc_inverse = norm_forward(start, enc_weights[0][0], enc_weights[1][0])
    enc_attn_in = enc_out.astype(jnp.bfloat16)
    enc_branch, enc_attn_kept = attend_forward(enc_attn_in, enc_attn_in, images, live, enc_weights)
    enc_middle = start + enc_weights[10][0] * enc_branch
    enc_feed, enc_feed_kept = feed_forward(enc_middle, enc_weights)
    latent_f = enc_middle + enc_weights[10][1] * enc_feed
    reg_weights = fetch(1, arrays)
    query_start = jnp.dot(pick_masked, pos_table, precision=highest)
    query_out, query_normed, query_inverse = norm_forward(
        query_start, reg_weights[0][0], reg_weights[1][0]
    )
    latent_out, latent_normed, latent_inverse = norm_forward(
        latent_f, reg_weights[0][0], reg_weights[1][0]
    )
    query_in = query_out.astype(jnp.bfloat16)
    key_in = jnp.concatenate(
        [
            latent_out.astype(jnp.bfloat16).reshape(images, SET, model),
            query_in.reshape(images, SET, model),
        ],
        axis=1,
    ).reshape(-1, model)
    key_live = jnp.concatenate([live, live])
    reg_branch, reg_attn_kept = attend_forward(query_in, key_in, images, key_live, reg_weights)
    reg_middle = query_start + reg_weights[10][0] * reg_branch
    reg_feed, reg_feed_kept = feed_forward(reg_middle, reg_weights)
    regressed_f = reg_middle + reg_weights[10][1] * reg_feed
    reg_back = fetch(1, arrays)
    grad_final = grad_out * live_rows
    reg_scale_late = jnp.sum(grad_final * reg_feed, axis=0)
    grad_from_feed, reg_gain_late, reg_shift_late, reg_feed_grads = feed_backward(
        reg_back[10][1] * grad_final, reg_feed_kept, reg_back
    )
    grad_reg_middle = grad_final + grad_from_feed
    reg_scale_early = jnp.sum(grad_reg_middle * reg_branch, axis=0)
    grad_query_in, grad_key_in, reg_attn_grads = attend_backward(
        reg_back[10][0] * grad_reg_middle, query_in, key_in, key_live, reg_attn_kept, reg_back
    )
    grad_key_in = grad_key_in.reshape(images, 2 * SET, model)
    grad_query_norm = grad_query_in + grad_key_in[:, SET:].reshape(-1, model)
    grad_latent_norm = grad_key_in[:, :SET].reshape(-1, model)
    back_query, reg_gain_query, reg_shift_query = norm_backward(
        grad_query_norm, query_normed, query_inverse, reg_back[0][0]
    )
    back_latent, reg_gain_key, reg_shift_key = norm_backward(
        grad_latent_norm, latent_normed, latent_inverse, reg_back[0][0]
    )
    grad_query_start = grad_reg_middle + back_query
    reg_grads = (
        (
            jnp.stack([reg_gain_query + reg_gain_key, reg_gain_late]),
            jnp.stack([reg_shift_query + reg_shift_key, reg_shift_late]),
        )
        + reg_attn_grads
        + reg_feed_grads
        + (jnp.stack([reg_scale_early, reg_scale_late]),)
    )
    reg_shards = (
        lax.psum_scatter(reg_grads[0], ("dp", "fsdp"), scatter_dimension=1, tiled=True),
        lax.psum_scatter(reg_grads[1], ("dp", "fsdp"), scatter_dimension=1, tiled=True),
        lax.psum_scatter(reg_grads[2], ("dp", "fsdp"), scatter_dimension=0, tiled=True),
        lax.psum_scatter(reg_grads[3], ("dp", "fsdp"), scatter_dimension=0, tiled=True),
        lax.psum_scatter(reg_grads[4], ("dp", "fsdp"), scatter_dimension=0, tiled=True),
        lax.psum_scatter(reg_grads[5], ("dp", "fsdp"), scatter_dimension=0, tiled=True),
        lax.psum_scatter(reg_grads[6], ("dp", "fsdp"), scatter_dimension=0, tiled=True),
        lax.psum_scatter(reg_grads[7], ("dp", "fsdp"), scatter_dimension=0, tiled=True),
        lax.psum_scatter(reg_grads[8], ("dp", "fsdp"), scatter_dimension=0, tiled=True),
        lax.psum_scatter(reg_grads[9], ("dp", "fsdp"), scatter_dimension=0, tiled=True),
        lax.psum_scatter(reg_grads[10], ("dp", "fsdp"), scatter_dimension=1, tiled=True),
    )
    enc_back = fetch(0, arrays)
    grad_finish = grad_latent * live_rows + back_latent
    enc_scale_late = jnp.sum(grad_finish * enc_feed, axis=0)
    grad_from_feed, enc_gain_late, enc_shift_late, enc_feed_grads = feed_backward(
        enc_back[10][1] * grad_finish, enc_feed_kept, enc_back
    )
    grad_enc_middle = grad_finish + grad_from_feed
    enc_scale_early = jnp.sum(grad_enc_middle * enc_branch, axis=0)
    grad_as_query, grad_as_key, enc_attn_grads = attend_backward(
        enc_back[10][0] * grad_enc_middle, enc_attn_in, enc_attn_in, live, enc_attn_kept, enc_back
    )
    back_start, enc_gain_early, enc_shift_early = norm_backward(
        grad_as_query + grad_as_key, enc_normed, enc_inverse, enc_back[0][0]
    )
    grad_start = grad_enc_middle + back_start
    grad_table = jnp.dot(pick_visible.T, grad_start, precision=highest) + jnp.dot(
        pick_masked.T, grad_query_start, precision=highest
    )
    enc_grads = (
        (jnp.stack([enc_gain_early, enc_gain_late]), jnp.stack([enc_shift_early, enc_shift_late]))
        + enc_attn_grads
        + enc_feed_grads
        + (jnp.stack([enc_scale_early, enc_scale_late]),)
    )
    enc_shards = (
        lax.psum_scatter(grad_table, ("dp", "fsdp"), scatter_dimension=1, tiled=True),
        lax.psum_scatter(enc_grads[0], ("dp", "fsdp"), scatter_dimension=1, tiled=True),
        lax.psum_scatter(enc_grads[1], ("dp", "fsdp"), scatter_dimension=1, tiled=True),
        lax.psum_scatter(enc_grads[2], ("dp", "fsdp"), scatter_dimension=0, tiled=True),
        lax.psum_scatter(enc_grads[3], ("dp", "fsdp"), scatter_dimension=0, tiled=True),
        lax.psum_scatter(enc_grads[4], ("dp", "fsdp"), scatter_dimension=0, tiled=True),
        lax.psum_scatter(enc_grads[5], ("dp", "fsdp"), scatter_dimension=0, tiled=True),
        lax.psum_scatter(enc_grads[6], ("dp", "fsdp"), scatter_dimension=0, tiled=True),
        lax.psum_scatter(enc_grads[7], ("dp", "fsdp"), scatter_dimension=0, tiled=True),
        lax.psum_scatter(enc_grads[8], ("dp", "fsdp"), scatter_dimension=0, tiled=True),
        lax.psum_scatter(enc_grads[9], ("dp", "fsdp"), scatter_dimension=0, tiled=True),
        lax.psum_scatter(enc_grads[10], ("dp", "fsdp"), scatter_dimension=1, tiled=True),
    )
    pos_shard = enc_shards[0]
    weight_shards = tuple(
        (jnp.stack([early, late]) for early, late in zip(enc_shards[1:], reg_shards))
    )
    return (
        latent_f.astype(jnp.bfloat16),
        regressed_f.astype(jnp.bfloat16),
        grad_start,
        pos_shard,
    ) + weight_shards


def solution(mesh):
    in_specs = (
        P(("dp", "fsdp"), None),
        P(("dp", "fsdp"), None),
        P(("dp", "fsdp"), None),
        P(("dp", "fsdp"), None),
        P(None, ("dp", "fsdp")),
        P(None, None, ("dp", "fsdp")),
        P(None, None, ("dp", "fsdp")),
        P(None, ("dp", "fsdp"), None),
        P(None, ("dp", "fsdp")),
        P(None, ("dp", "fsdp"), None),
        P(None, ("dp", "fsdp")),
        P(None, ("dp", "fsdp"), None),
        P(None, ("dp", "fsdp")),
        P(None, ("dp", "fsdp"), None),
        P(None, ("dp", "fsdp")),
        P(None, None, ("dp", "fsdp")),
    )
    out_specs = (
        P(("dp", "fsdp"), None),
        P(("dp", "fsdp"), None),
        P(("dp", "fsdp"), None),
        P(None, ("dp", "fsdp")),
        P(None, None, ("dp", "fsdp")),
        P(None, None, ("dp", "fsdp")),
        P(None, ("dp", "fsdp"), None),
        P(None, ("dp", "fsdp")),
        P(None, ("dp", "fsdp"), None),
        P(None, ("dp", "fsdp")),
        P(None, ("dp", "fsdp"), None),
        P(None, ("dp", "fsdp")),
        P(None, ("dp", "fsdp"), None),
        P(None, ("dp", "fsdp")),
        P(None, None, ("dp", "fsdp")),
    )
    return jax.shard_map(local, mesh=mesh, in_specs=in_specs, out_specs=out_specs, check_vma=False)
```

profile of v0, /device:TPU:0, one launch (start us, length us, event | category | flops | bytes accessed | tf_op | source)
XLA Modules:
  0.0 1873.8 jit_solution(8411038986088732026)
XLA Ops:
  18.0 42.3 %all-reduce.24 = (bf16[768]{0:T(1024)(128)(2,1)S(1)}, bf16[1536]{0:T(1024)(128)(2,1)S(1)}, bf16[3072]{0:T(1024)(128)(2,1)S(1)}, bf16[768]{0:T(1024)(128)(2,1)S(1...) all-reduce(bf16[768]{0:T(1024)(128)(2,1)S(1)} %dynamic-update-slice, ...), channel_id=8, replica_groups=mesh['dp'=8,'fsdp'=4] {'dp','fsdp'}, use_global_device_ids=true, to_apply=%add.2 | all-reduce | flops 12288 | bytes 49152
  61.1 41.7 %all-gather.1 = bf16[1,2,768]{1,0,2:T(2,128)(2,1)S(1)} all-gather(bf16[1,2,24]{1,0,2:T(2,128)(2,1)S(1)} %copy.198), channel_id=3, replica_groups=mesh['dp'=8,'fsdp'=4] {'dp','fsdp'}, dimensions={2}, use_global_device_ids=true | all-gather | bytes 3168 | tf_op jit(solution)/shard_map/all_gather | solution.py:241
  103.2 4.6 slice_reduce_fusion.7
  107.8 38.4 %all-gather.2 = bf16[1,2,768]{1,0,2:T(2,128)(2,1)S(1)} all-gather(bf16[1,2,24]{1,0,2:T(2,128)(2,1)S(1)} %copy.199), channel_id=4, replica_groups=mesh['dp'=8,'fsdp'=4] {'dp','fsdp'}, dimensions={2}, use_global_device_ids=true | all-gather | bytes 3168 | tf_op jit(solution)/shard_map/all_gather | solution.py:242
  146.6 4.6 slice_reduce_fusion.6
  151.2 39.7 %all-gather = bf16[1,2,768]{1,0,2:T(2,128)(2,1)S(1)} all-gather(bf16[1,2,24]{1,0,2:T(2,128)(2,1)S(1)} %copy.197), channel_id=2, replica_groups=mesh['dp'=8,'fsdp'=4] {'dp','fsdp'}, dimensions={2}, use_global_device_ids=true | all-gather | bytes 3168 | tf_op jit(solution)/shard_map/all_gather | solution.py:251
  191.3 4.6 slice_reduce_fusion.8
  195.9 38.8 %all-gather.12 = bf16[1,2,768]{1,0,2:T(2,128)(2,1)S(1)} all-gather(bf16[1,2,24]{1,0,2:T(2,128)(2,1)S(1)} %copy.201), channel_id=14, replica_groups=mesh['dp'=8,'fsdp'=4] {'dp','fsdp'}, dimensions={2}, use_global_device_ids=true | all-gather | bytes 3168 | tf_op jit(solution)/shard_map/all_gather | solution.py:52
  235.1 4.6 slice_reduce_fusion.1
  239.6 39.6 %all-gather.13 = bf16[1,2,768]{1,0,2:T(2,128)(2,1)S(1)} all-gather(bf16[1,2,24]{1,0,2:T(2,128)(2,1)S(1)} %copy.202), channel_id=15, replica_groups=mesh['dp'=8,'fsdp'=4] {'dp','fsdp'}, dimensions={2}, use_global_device_ids=true | all-gather | bytes 3168 | tf_op jit(solution)/shard_map/all_gather | solution.py:53
  279.7 4.6 slice_reduce_fusion
  284.3 38.5 %all-gather.11 = bf16[1,2,768]{1,0,2:T(2,128)(2,1)S(1)} all-gather(bf16[1,2,24]{1,0,2:T(2,128)(2,1)S(1)} %copy.200), channel_id=13, replica_groups=mesh['dp'=8,'fsdp'=4] {'dp','fsdp'}, dimensions={2}, use_global_device_ids=true | all-gather | bytes 3168 | tf_op jit(solution)/shard_map/all_gather | solution.py:62
  323.2 4.6 slice_reduce_fusion.2
  327.7 39.3 %all_gather.81 = bf16[196,768]{0,1:T(8,128)(2,1)S(1)} all-gather(bf16[196,24]{0,1:T(8,128)(2,1)S(1)} %copy-done.65), channel_id=1, replica_groups=mesh['dp'=8,'fsdp'=4] {'dp','fsdp'}, dimensions={1}, use_global_device_ids=true | all-gather | bytes 310464 | tf_op jit(solution)/shard_map/all_gather | solution.py:240
  373.0 5.0 fusion.49
  406.3 4.1 fusion.166
  412.2 8.1 fusion.30
  420.3 9.8 fusion.165
  440.3 4.8 fusion.45
  452.6 3.9 fusion.34
  459.0 3.9 reshape.294
  472.4 3.6 fusion.164
  477.5 8.3 fusion.22
  485.8 28.8 %all-gather.45.cloned.1.call-done = bf16[1,3072,768]{2,1,0:T(8,128)(2,1)} async-done(((bf16[1,96,768]{2,1,0:T(8,128)(2,1)}), bf16[1,3072,768]{2,1,0:T(8,128)(2,1)}) %all-gather.45.cloned.1.call-update) | async-done | bytes 4718608 | tf_op jit(solution)/shard_map/all_gather | solution.py:60
  514.6 9.9 convert_reduce_fusion
  530.7 5.3 multiply_reduce_fusion.2
  542.0 4.3 convert_reduce_fusion.2
  566.3 3.6 multiply_reduce_fusion.7
  570.8 7.2 convert_reduce_fusion.1
  578.0 5.6 multiply_reduce_fusion.8
  613.3 3.5 fusion.107
  616.9 3.6 fusion.110
  622.9 4.6 fusion.179
  638.6 10.3 fusion.163
  649.0 10.3 fusion.162
  660.1 9.0 fusion.160
  669.7 8.9 fusion.161
  679.3 3.9 fusion.58
  686.4 58.6 %all-reduce.27.cloned.1.call-done = (f32[2,768]{1,0:T(2,128)}, f32[2,768]{1,0:T(2,128)}, f32[2,768]{1,0:T(2,128)}, f32[2,768]{1,0:T(2,128)}, f32[1536]{0:T(1024)...) async-done(((f32[2,768]{1,0:T(2,128)}, f32[2,768]{1,0:T(2,128)}, ...) | async-done | bytes 86032
  759.6 90.6 %reduce-scatter.24.cloned.1.call-done = f32[24,768]{1,0:T(8,128)} async-done(((f32[768,768]{1,0:T(8,128)}), f32[24,768]{1,0:T(8,128)}) %reduce-scatter.24.cloned.1.call-update) | async-done | bytes 73744 | tf_op jit(solution)/shard_map/reduce_scatter | solution.py:318
  850.2 104.2 %reduce-scatter.22.cloned.1.call-done = f32[24,768]{1,0:T(8,128)} async-done(((f32[768,768]{1,0:T(8,128)}), f32[24,768]{1,0:T(8,128)}) %reduce-scatter.22.cloned.1.call-update) | async-done | bytes 73744 | tf_op jit(solution)/shard_map/reduce_scatter | solution.py:356
  956.0 122.1 %reduce-scatter.20.cloned.1.call-done = f32[24,2304]{1,0:T(8,128)} async-done(((f32[768,2304]{1,0:T(8,128)}), f32[24,2304]{1,0:T(8,128)}) %reduce-scatter.20.cloned.1.call-update) | async-done | bytes 221200 | tf_op jit(solution)/shard_map/reduce_scatter | solution.py:316
  1078.1 125.0 %reduce-scatter.18.cloned.1.call-done = f32[24,2304]{1,0:T(8,128)} async-done(((f32[768,2304]{1,0:T(8,128)}), f32[24,2304]{1,0:T(8,128)}) %reduce-scatter.18.cloned.1.call-update) | async-done | bytes 221200 | tf_op jit(solution)/shard_map/reduce_scatter | solution.py:354
  1205.0 138.8 %reduce-scatter.32.cloned.1.call-done = f32[96,768]{1,0:T(8,128)} async-done(((f32[3072,768]{1,0:T(8,128)}), f32[96,768]{1,0:T(8,128)}) %reduce-scatter.32.cloned.1.call-update) | async-done | bytes 294928 | tf_op jit(solution)/shard_map/reduce_scatter | solution.py:322
  1343.8 141.4 %reduce-scatter.30.cloned.1.call-done = f32[96,768]{1,0:T(8,128)} async-done(((f32[3072,768]{1,0:T(8,128)}), f32[96,768]{1,0:T(8,128)}) %reduce-scatter.30.cloned.1.call-update) | async-done | bytes 294928 | tf_op jit(solution)/shard_map/reduce_scatter | solution.py:360
  1487.1 138.4 %reduce-scatter.26.cloned.1.call-done = f32[24,3072]{1,0:T(8,128)} async-done(((f32[768,3072]{1,0:T(8,128)}), f32[24,3072]{1,0:T(8,128)}) %reduce-scatter.26.cloned.1.call-update) | async-done | bytes 294928 | tf_op jit(solution)/shard_map/reduce_scatter | solution.py:358
  1625.5 141.4 %reduce-scatter.28.cloned.1.call-done = f32[24,3072]{1,0:T(8,128)} async-done(((f32[768,3072]{1,0:T(8,128)}), f32[24,3072]{1,0:T(8,128)}) %reduce-scatter.28.cloned.1.call-update) | async-done | bytes 294928 | tf_op jit(solution)/shard_map/reduce_scatter | solution.py:320
  1768.8 98.0 %reduce-scatter.16.cloned.1.call-done = f32[196,24]{0,1:T(8,128)} async-done(((f32[196,768]{0,1:T(8,128)}), f32[196,24]{0,1:T(8,128)}) %reduce-scatter.16.cloned.1.call-update) | async-done | bytes 18832 | tf_op jit(solution)/shard_map/reduce_scatter | solution.py:351
  (439 shorter events, 182.9 us)
Async XLA Ops:
  7.2 9.0 copy-start.78
  7.2 8.7 copy-start.75
  7.2 8.8 copy-start.76
  7.2 8.8 copy-start.71
  7.2 8.8 copy-start.72
  7.2 8.8 copy-start.73
  7.3 8.8 copy-start.74
  7.3 8.8 copy-start.77
  7.3 8.8 copy-start.70
  7.3 365.7 %all-gather.31.cloned.1.call-start = ((), (), s32[]{:S(2)}) async-start(), calls=%async_computation.18 | async-start | bytes 3649536 | tf_op jit(solution)/shard_map/all_gather | solution.py:243
  9.1 397.3 %all-gather.33.cloned.1.call-start = ((), (), s32[]{:S(2)}) async-start(), calls=%async_computation.19 | async-start | bytes 1216512 | tf_op jit(solution)/shard_map/all_gather | solution.py:245
  10.6 401.6 %all-gather.35.cloned.1.call-start = ((), (), s32[]{:S(2)}) async-start(), calls=%async_computation.20 | async-start | bytes 4866048 | tf_op jit(solution)/shard_map/all_gather | solution.py:247
  12.4 408.0 %all-gather.37.cloned.1.call-start = ((), (), s32[]{:S(2)}) async-start(), calls=%async_computation.21 | async-start | bytes 4866048 | tf_op jit(solution)/shard_map/all_gather | solution.py:249
  13.2 418.7 %all-gather.39.cloned.1.call-start = ((), (), s32[]{:S(2)}) async-start(), calls=%async_computation.22 | async-start | bytes 3649536 | tf_op jit(solution)/shard_map/all_gather | solution.py:54
  13.8 458.6 %all-gather.41.cloned.1.call-start = ((), (), s32[]{:S(2)}) async-start(), calls=%async_computation.23 | async-start | bytes 1216512 | tf_op jit(solution)/shard_map/all_gather | solution.py:56
  14.3 463.1 %all-gather.43.cloned.1.call-start = ((), (), s32[]{:S(2)}) async-start(), calls=%async_computation.24 | async-start | bytes 4866048 | tf_op jit(solution)/shard_map/all_gather | solution.py:58
  15.1 499.5 %all-gather.45.cloned.1.call-start = ((), (), s32[]{:S(2)}) async-start(), calls=%async_computation.25 | async-start | bytes 4866048 | tf_op jit(solution)/shard_map/all_gather | solution.py:60
  15.8 729.2 %all-reduce.27.cloned.1.call-start = ((), (), s32[]{:S(2)}) async-start(), calls=%async_computation.26 | async-start | bytes 188416
  15.9 352.4 %copy-start.63 = (pred[512]{0:T(512)(128)(4,1)}, pred[512]{0:T(512)(128)(4,1)S(1)}, u32[]{:S(2)}) copy-start(pred[512]{0:T(512)(128)(4,1)S(1)} %get-tuple-element.120) | copy-start | bytes 1540
  16.2 352.1 %copy-start.57 = (s32[512]{0:T(512)}, s32[512]{0:T(512)S(1)}, u32[]{:S(2)}) copy-start(s32[512]{0:T(512)S(1)} %select_bitcast_fusion) | copy-start | bytes 6148
  16.2 350.8 %copy-start.61 = (s32[512]{0:T(512)}, s32[512]{0:T(512)S(1)}, u32[]{:S(2)}) copy-start(s32[512]{0:T(512)S(1)} %pad_bitcast_fusion) | copy-start | bytes 6148
  107.7 264.0 %copy-start.53 = (f32[768]{0:T(1024)}, f32[768]{0:T(1024)S(1)}, u32[]{:S(2)}) copy-start(f32[768]{0:T(1024)S(1)} %get-tuple-element.44) | copy-start | bytes 9220
  151.2 261.0 %copy-start.66 = (f32[768]{0:T(1024)}, f32[768]{0:T(1024)S(1)}, u32[]{:S(2)}) copy-start(f32[768]{0:T(1024)S(1)} %get-tuple-element.45) | copy-start | bytes 9220
  279.6 48.1 %copy-start.65 = (bf16[196,24]{0,1:T(8,128)(2,1)S(1)}, bf16[196,24]{0,1:T(8,128)(2,1)}, u32[]{:S(2)}) copy-start(bf16[196,24]{0,1:T(8,128)(2,1)} %param.20) | copy-start | bytes 28228
  284.2 193.2 %copy-start.68 = (f32[768]{0:T(1024)}, f32[768]{0:T(1024)S(1)}, u32[]{:S(2)}) copy-start(f32[768]{0:T(1024)S(1)} %get-tuple-element.39) | copy-start | bytes 9220
  368.0 104.4 %copy-start.1 = (f32[512,768]{1,0:T(8,128)}, f32[512,768]{1,0:T(8,128)S(1)}, u32[]{:S(2)}) copy-start(f32[512,768]{1,0:T(8,128)S(1)} %get-tuple-element.136) | copy-start | bytes 4718596
  369.3 37.0 %copy-start.5 = (f32[512,768]{1,0:T(8,128)}, f32[512,768]{1,0:T(8,128)S(1)}, u32[]{:S(2)}) copy-start(f32[512,768]{1,0:T(8,128)S(1)} %get-tuple-element.130) | copy-start | bytes 4718596
  431.8 8.4 copy-start.15
  452.6 10.4 copy-start.11
  477.5 37.1 %copy-start.47 = (bf16[512,768]{1,0:T(8,128)(2,1)S(1)}, bf16[512,768]{1,0:T(8,128)(2,1)}, u32[]{:S(2)}) copy-start(bf16[512,768]{1,0:T(8,128)(2,1)} %get-tuple-element.82) | copy-start | bytes 2359300
  514.6 9.9 copy-start.21
  514.6 9.9 copy-start.80
  539.0 7.3 slice-start
  555.3 15.4 slice-start.4
  555.3 15.4 slice-start.6
  560.2 10.5 slice-start.5
  560.2 10.5 slice-start.7
  566.3 11.6 slice-start.2
  570.7 7.2 copy-start.48
  613.3 236.9 %reduce-scatter.24.cloned.1.call-start = ((), (), s32[]{:S(2)}) async-start(), calls=%async_computation.13 | async-start | bytes 2433024 | tf_op jit(solution)/shard_map/reduce_scatter | solution.py:318
  616.9 337.5 %reduce-scatter.22.cloned.1.call-start = ((), (), s32[]{:S(2)}) async-start(), calls=%async_computation.12 | async-start | bytes 2433024 | tf_op jit(solution)/shard_map/reduce_scatter | solution.py:356
  620.6 457.6 %reduce-scatter.20.cloned.1.call-start = ((), (), s32[]{:S(2)}) async-start(), calls=%async_computation.11 | async-start | bytes 7299072 | tf_op jit(solution)/shard_map/reduce_scatter | solution.py:316
  630.9 572.3 %reduce-scatter.18.cloned.1.call-start = ((), (), s32[]{:S(2)}) async-start(), calls=%async_computation.10 | async-start | bytes 7299072 | tf_op jit(solution)/shard_map/reduce_scatter | solution.py:354
  638.2 705.6 %reduce-scatter.32.cloned.1.call-start = ((), (), s32[]{:S(2)}) async-start(), calls=%async_computation.17 | async-start | bytes 9732096 | tf_op jit(solution)/shard_map/reduce_scatter | solution.py:322
  649.0 836.2 %reduce-scatter.30.cloned.1.call-start = ((), (), s32[]{:S(2)}) async-start(), calls=%async_computation.16 | async-start | bytes 9732096 | tf_op jit(solution)/shard_map/reduce_scatter | solution.py:360
  659.4 966.1 %reduce-scatter.26.cloned.1.call-start = ((), (), s32[]{:S(2)}) async-start(), calls=%async_computation.14 | async-start | bytes 9732096 | tf_op jit(solution)/shard_map/reduce_scatter | solution.py:358
  669.0 1097.9 %reduce-scatter.28.cloned.1.call-start = ((), (), s32[]{:S(2)}) async-start(), calls=%async_computation.15 | async-start | bytes 9732096 | tf_op jit(solution)/shard_map/reduce_scatter | solution.py:320
  678.6 1188.2 %reduce-scatter.16.cloned.1.call-start = ((), (), s32[]{:S(2)}) async-start(), calls=%async_computation.9 | async-start | bytes 811008 | tf_op jit(solution)/shard_map/reduce_scatter | solution.py:351
  (63 other events, 168.9 us)
Sparse Core Ops, SparseCore 0:
  11.6 63.0 all-gather.30
  77.6 53.2 all-gather.32
  134.4 63.0 all-gather.34
  200.8 63.5 all-gather.36
  267.2 59.9 all-gather.38
  329.9 52.6 all-gather.40
  386.1 62.5 all-gather.42
  452.1 62.4 all-gather.44
  613.4 131.6 all-reduce.26
  750.2 99.9 reduce-scatter.23
  856.3 98.0 reduce-scatter.21
  959.9 118.1 reduce-scatter.19
  1084.7 118.3 reduce-scatter.17
  1208.9 134.7 reduce-scatter.31
  1350.5 134.6 reduce-scatter.29
  1490.9 134.5 reduce-scatter.25
  1632.3 134.6 reduce-scatter.27
  1772.5 94.2 reduce-scatter.15
where the time goes:
time: 1880 us; the launch traced here: 1870 us
  waiting for transfers between devices  1190 us (63%)
  blocking collectives  318 us (17%)
  matrix products  184 us (10%)
  local copies, waits for them, and re-layouts  114 us (6%)
  other arithmetic  50.2 us (3%)
    reduce_scatter x1, waiting for transfers between devices, local(): lax.psum_scatter(enc_grads[8], ('dp', 'fsdp'), scatter_dimension=0, tiled...  141 us
    reduce_scatter x1, waiting for transfers between devices, local(): lax.psum_scatter(reg_grads[6], ('dp', 'fsdp'), scatter_dimension=0, tiled...  141 us
    reduce_scatter x1, waiting for transfers between devices, local(): lax.psum_scatter(reg_grads[8], ('dp', 'fsdp'), scatter_dimension=0, tiled...  139 us
    reduce_scatter x1, waiting for transfers between devices, local(): lax.psum_scatter(enc_grads[6], ('dp', 'fsdp'), scatter_dimension=0, tiled...  138 us
    reduce_scatter x1, waiting for transfers between devices, local(): lax.psum_scatter(enc_grads[2], ('dp', 'fsdp'), scatter_dimension=0, tiled...  125 us
    reduce_scatter x1, waiting for transfers between devices, local(): lax.psum_scatter(reg_grads[2], ('dp', 'fsdp'), scatter_dimension=0, tiled...  122 us
    reduce_scatter x1, waiting for transfers between devices, local(): lax.psum_scatter(enc_grads[4], ('dp', 'fsdp'), scatter_dimension=0, tiled...  104 us
    reduce_scatter x1, waiting for transfers between devices, local(): lax.psum_scatter(grad_table, ('dp', 'fsdp'), scatter_dimension=1, tiled=T...  98 us
  transfers between devices with their start and end apart: 18, of which 11 were waited for; matrix products, arithmetic and copies ran while one was open for 13% of the time, Pallas kernels for 0%

commit v1 on v0

--- a/solution.py
+++ b/solution.py
@@ -4,12 +4,325 @@
 import jax
 import jax.numpy as jnp
 from jax import lax
+from jax.experimental import pallas as pl
+from jax.experimental.pallas import tpu as pltpu
 from jax.sharding import PartitionSpec as P
 
 HEAD_DIM = 64
 VIS = 98
 SET = 128
 PATCHES = 196
+
+
+MESH = pl.DeviceIdType.MESH
+WIDE = jnp.float32
+LOW = jnp.bfloat16
+
+
+def lanes(start, size):
+    return pl.ds(pl.multiple_of(start, 128), size)
+
+
+class Place:
+    def __init__(self, line):
+        dp, fsdp = lax.axis_index("dp"), lax.axis_index("fsdp")
+        self.line = line
+        self.z, self.y = dp // 2, dp % 2
+        self.x, self.core = fsdp // 2, fsdp % 2
+        z, y, x, core = self.z, self.y, self.x, self.core
+        first_y = jnp.where(core == 0, 1 - y, y)
+        first_x = jnp.where(core == 0, x, 1 - x)
+        second_y = jnp.where(core == 0, y, 1 - y)
+        second_x = jnp.where(core == 0, 1 - x, x)
+        self.own = 2 * y + x
+        self.first = 2 * first_y + first_x
+        self.second = 2 * second_y + second_x
+        self.across = 2 * (1 - y) + (1 - x)
+        self.twin = self.at(z, y, x, 1 - core)
+        self.near = self.at(z, first_y, first_x, core)
+        self.far = self.at(z, second_y, second_x, core)
+        self.above = [
+            self.at(lax.rem(z + step, line), y, x, core) for step in range(1, line)
+        ]
+
+    def at(self, z, y, x, core):
+        return (2 * z + y, 2 * x + core)
+
+    def greet(self):
+        barrier = pltpu.get_barrier_semaphore()
+        others = [self.twin, self.near, self.far] + self.above
+        for other in others:
+            pl.semaphore_signal(barrier, inc=1, device_id=other, device_id_type=MESH)
+        pl.semaphore_wait(barrier, len(others))
+
+
+class Copies:
+    def __init__(self, send, recv):
+        self.send, self.recv, self.used, self.sent = send, recv, 0, []
+
+    def remote(self, source, target, device):
+        copy = pltpu.make_async_remote_copy(
+            src_ref=source,
+            dst_ref=target,
+            send_sem=self.send.at[self.used],
+            recv_sem=self.recv.at[self.used],
+            device_id=device,
+            device_id_type=MESH,
+        )
+        self.used += 1
+        copy.start()
+        self.sent.append(copy)
+        return copy
+
+    def local(self, source, target):
+        copy = pltpu.make_async_copy(source, target, self.send.at[self.used])
+        self.used += 1
+        copy.start()
+        return copy
+
+    def drain(self):
+        for copy in self.sent:
+            copy.wait_send()
+
+
+def gather_body(line, items, *refs):
+    count = len(items)
+    shards, fulls = refs[:count], refs[count : 2 * count]
+    theirs, stages = refs[2 * count : 3 * count], refs[3 * count : 4 * count]
+    send, recv = refs[4 * count :]
+    place = Place(line)
+    copies = Copies(send, recv)
+    place.greet()
+    swaps = [copies.remote(shards[i], theirs[i], place.twin) for i in range(count)]
+    halves = [shape[2] // 2 for shape in items]
+    columns = [lanes(place.core * half, half) for half in halves]
+
+    def stage(i):
+        swaps[i].wait_recv()
+        rows = items[i][1]
+        for which, (low_ref, high_ref) in ((0, (shards[i], theirs[i])), (1, (theirs[i], shards[i]))):
+            @pl.when(place.core == which)
+            def _():
+                part = pl.ds(which * halves[i], halves[i])
+                both = jnp.concatenate(
+                    [low_ref[:, part].astype(WIDE), high_ref[:, part].astype(WIDE)], axis=0
+                )
+                stages[i][...] = both.astype(LOW)
+
+    def group(i, which):
+        return fulls[i].at[:, which, :, columns[i]]
+
+    def spread(i):
+        target = fulls[i].at[place.z, place.own, :, columns[i]]
+        own = copies.local(stages[i], target)
+        return [own] + [copies.remote(stages[i], target, device) for device in place.above]
+
+    def settle(i, started):
+        started[0].wait()
+        for copy in started[1:]:
+            copy.wait_recv()
+
+    def send_on(i, which, devices):
+        return [copies.remote(group(i, which), group(i, which), device) for device in devices]
+
+    ahead = 2
+    spreads = {}
+    last = []
+    for i in range(min(ahead, count)):
+        stage(i)
+        spreads[i] = spread(i)
+    own_sends = {}
+    for i in range(count):
+        settle(i, spreads[i])
+        own_sends[i] = send_on(i, place.own, [place.near, place.far, place.twin])
+        if i + ahead < count:
+            stage(i + ahead)
+            spreads[i + ahead] = spread(i + ahead)
+        near, far, twin = own_sends[i]
+        near.wait_recv()
+        onward = send_on(i, place.first, [place.far, place.twin])
+        last.append((far, twin, onward))
+        if i >= 1:
+            finish = last[i - 1]
+            finish[0].wait_recv()
+            finish[2][0].wait_recv()
+            more = send_on(i - 1, place.second, [place.twin]) + send_on(i - 1, place.across, [place.twin])
+            last[i - 1] = [finish[1], finish[2][1]] + more
+    finish = last[count - 1]
+    finish[0].wait_recv()
+    finish[2][0].wait_recv()
+    more = send_on(count - 1, place.second, [place.twin]) + send_on(count - 1, place.across, [place.twin])
+    last[count - 1] = [finish[1], finish[2][1]] + more
+    for group_last in last:
+        for copy in group_last:
+            copy.wait_recv()
+    copies.drain()
+
+
+def gather_all(shards, line):
+    items = [shard.shape for shard in shards]
+    items = [(line, 2 * rows, wide) for rows, wide in items]
+    total = len(items) * (1 + line + 3 + 2 + 2)
+    return pl.pallas_call(
+        functools.partial(gather_body, line, items),
+        out_shape=[jax.ShapeDtypeStruct((line, 4, rows, wide), LOW) for _, rows, wide in items],
+        in_specs=[pl.BlockSpec(memory_space=pltpu.VMEM)] * len(items),
+        out_specs=[pl.BlockSpec(memory_space=pl.ANY)] * len(items),
+        scratch_shapes=[pltpu.VMEM(shard.shape, LOW) for shard in shards]
+        + [pltpu.VMEM((rows, wide // 2), LOW) for _, rows, wide in items]
+        + [pltpu.SemaphoreType.DMA((total,)), pltpu.SemaphoreType.DMA((total,))],
+        name="gather_all",
+        compiler_params=pltpu.CompilerParams(
+            collective_id=0, has_side_effects=True, vmem_limit_bytes=24 << 20
+        ),
+    )(*shards)
+
+
+def reduce_body(line, items, *refs):
+    count = len(items)
+    grads, outs = refs[:count], refs[count : 2 * count]
+    per = 9
+    scratch = refs[2 * count : 2 * count + per * count]
+    send, recv = refs[2 * count + per * count :]
+    place = Place(line)
+    copies = Copies(send, recv)
+    place.greet()
+
+    def buffers(i):
+        return scratch[per * i : per * (i + 1)]
+
+    def begin(i):
+        mine, twins = buffers(i)[:2]
+        half = items[i][2] // 2
+        away = copies.remote(
+            grads[i].at[:, :, :, lanes((1 - place.core) * half, half)], twins, place.twin
+        )
+        here = copies.local(grads[i].at[:, :, :, lanes(place.core * half, half)], mine)
+        return away, here
+
+    def pair_add(i, started):
+        mine, twins = buffers(i)[:2]
+        started[0].wait_recv()
+        started[1].wait()
+
+        def step(k, _):
+            a, b = k // 4, k % 4
+            mine[a, b] = (mine[a, b].astype(WIDE) + twins[a, b].astype(WIDE)).astype(LOW)
+            return 0
+
+        lax.fori_loop(0, line * 4, step, 0)
+
+    def scatter_far(i):
+        mine, _, through, direct = buffers(i)[:4]
+        return [
+            copies.remote(mine.at[:, place.across], through, place.far),
+            copies.remote(mine.at[:, place.second], direct, place.far),
+        ]
+
+    def scatter_near(i, started):
+        mine, _, through, _, joined = buffers(i)[:5]
+        started[0].wait_recv()
+
+        def step(k, _):
+            through[k] = (through[k].astype(WIDE) + mine[k, place.first].astype(WIDE)).astype(LOW)
+            return 0
+
+        lax.fori_loop(0, line, step, 0)
+        return copies.remote(through, joined, place.near)
+
+    def scatter_line(i, far, near):
+        mine, _, _, direct, joined, owned, arrived = buffers(i)[:7]
+        far[1].wait_recv()
+        near.wait_recv()
+
+        def step(k, _):
+            owned[k] = (
+                mine[k, place.own].astype(WIDE) + direct[k].astype(WIDE) + joined[k].astype(WIDE)
+            ).astype(LOW)
+            return 0
+
+        lax.fori_loop(0, line, step, 0)
+        return [
+            copies.remote(
+                owned.at[lax.rem(place.z + step + 1, line)], arrived.at[step], place.above[step]
+            )
+            for step in range(line - 1)
+        ]
+
+    def swap(i, started):
+        owned, arrived, final, other = buffers(i)[5:]
+        for copy in started:
+            copy.wait_recv()
+        total = owned[place.z].astype(WIDE)
+        for step in range(line - 1):
+            total = total + arrived[step].astype(WIDE)
+        final[...] = total
+        rows = items[i][1] // 2
+        return copies.remote(
+            final.at[pl.ds(pl.multiple_of((1 - place.core) * rows, 8), rows)], other, place.twin
+        )
+
+    def finish(i, started):
+        final, other = buffers(i)[7:]
+        rows, half = items[i][1] // 2, items[i][2] // 2
+        outs[i][:, lanes(place.core * half, half)] = final[
+            pl.ds(pl.multiple_of(place.core * rows, 8), rows)
+        ]
+        started.wait_recv()
+        outs[i][:, lanes((1 - place.core) * half, half)] = other[...]
+
+    begun, far, near, lined, swapped = {}, {}, {}, {}, {}
+    for i in range(min(2, count)):
+        begun[i] = begin(i)
+    for t in range(count + 4):
+        if t < count:
+            pair_add(t, begun[t])
+            far[t] = scatter_far(t)
+            if t + 2 < count:
+                begun[t + 2] = begin(t + 2)
+        if 0 <= t - 1 < count:
+            near[t - 1] = scatter_near(t - 1, far[t - 1])
+        if 0 <= t - 2 < count:
+            lined[t - 2] = scatter_line(t - 2, far[t - 2], near[t - 2])
+        if 0 <= t - 3 < count:
+            swapped[t - 3] = swap(t - 3, lined[t - 3])
+        if 0 <= t - 4 < count:
+            finish(t - 4, swapped[t - 4])
+    copies.drain()
+
+
+def reduce_all(grads, line):
+    items = [(line, grad.shape[0] // (4 * line), grad.shape[1]) for grad in grads]
+    views = [
+        grad.reshape(line, 4, rows, wide) for grad, (_, rows, wide) in zip(grads, items)
+    ]
+    scratch = []
+    for _, rows, wide in items:
+        half = wide // 2
+        scratch += [
+            pltpu.VMEM((line, 4, rows, half), LOW),
+            pltpu.VMEM((line, 4, rows, half), LOW),
+            pltpu.VMEM((line, rows, half), LOW),
+            pltpu.VMEM((line, rows, half), LOW),
+            pltpu.VMEM((line, rows, half), LOW),
+            pltpu.VMEM((line, rows, half), LOW),
+            pltpu.VMEM((line - 1, rows, half), LOW),
+            pltpu.VMEM((rows, half), WIDE),
+            pltpu.VMEM((rows // 2, half), WIDE),
+        ]
+    total = len(items) * (line + 5)
+    return pl.pallas_call(
+        functools.partial(reduce_body, line, items),
+        out_shape=[jax.ShapeDtypeStruct((rows // 2, wide), WIDE) for _, rows, wide in items],
+        in_specs=[pl.BlockSpec(memory_space=pl.ANY)] * len(items),
+        out_specs=[pl.BlockSpec(memory_space=pltpu.VMEM)] * len(items),
+        scratch_shapes=scratch
+        + [pltpu.SemaphoreType.DMA((total,)), pltpu.SemaphoreType.DMA((total,))],
+        name="reduce_all",
+        compiler_params=pltpu.CompilerParams(
+            collective_id=1, has_side_effects=True, vmem_limit_bytes=60 << 20
+        ),
+    )(*views)
 
 
 def norm_forward(value, gain, shift):
@@ -191,7 +504,58 @@
     return (grad_middle, grad_gain, grad_shift, (grad_w_fc1, grad_b_fc1, grad_w_fc2, grad_b_fc2))
 
 
+def pack(pos, ln_gain, ln_bias, scales, b_proj, b_fc2, b_qkv, b_fc1):
+    rows = pos.shape[1]
+
+    def turned(array):
+        return jnp.moveaxis(array.reshape(-1, array.shape[-1]), 1, 0)
+
+    def folded(array):
+        return turned(array.reshape(2, -1, rows))
+
+    columns = [turned(pos), turned(ln_gain), turned(ln_bias), turned(scales)]
+    columns += [turned(b_proj), turned(b_fc2), folded(b_qkv), folded(b_fc1)]
+    joined = jnp.concatenate([column.astype(LOW) for column in columns], axis=1)
+    return jnp.pad(joined, ((0, 0), (0, 256 - joined.shape[1])))
+
+
+def unpack_rows(extra, patches, devices, fold):
+    at = patches
+    turned = extra.T
+    pos = turned[:patches]
+    outs = []
+    for _ in range(3):
+        outs.append(turned[at : at + 4].reshape(2, 2, -1))
+        at += 4
+    for _ in range(2):
+        outs.append(turned[at : at + 2])
+        at += 2
+    for pieces in fold:
+        part = turned[at : at + 2 * pieces].reshape(2, pieces, devices, -1)
+        outs.append(jnp.swapaxes(part, 1, 2).reshape(2, -1))
+        at += 2 * pieces
+    return [pos] + outs
+
+
+def repack(pos, ln_gain, ln_bias, scales, b_proj, b_fc2, b_qkv, b_fc1, devices):
+    rows = pos.shape[1] // devices
+
+    def turned(array):
+        return jnp.moveaxis(array.reshape(-1, array.shape[-1]), 1, 0)
+
+    def folded(array):
+        part = jnp.swapaxes(array.reshape(2, devices, -1, rows), 1, 2)
+        return turned(part.reshape(-1, devices * rows))
+
+    columns = [turned(pos), turned(ln_gain), turned(ln_bias), turned(scales)]
+    columns += [turned(b_proj), turned(b_fc2), folded(b_qkv), folded(b_fc1)]
+    joined = jnp.concatenate([column.astype(LOW) for column in columns], axis=1)
+    return jnp.pad(joined, ((0, 0), (0, 256 - joined.shape[1])))
+
+
 def local(
+    kernels,
+    devices,
     patches,
     order,
     grad_latent,
@@ -236,22 +600,43 @@
 
     pick_visible = picker(order[:, :VIS])
     pick_masked = picker(order[:, VIS:])
-    gathered = (
-        lax.all_gather(pos_embed, ("dp", "fsdp"), axis=1, tiled=True),
-        lax.all_gather(ln_gain[0], ("dp", "fsdp"), axis=1, tiled=True),
-        lax.all_gather(ln_bias[0], ("dp", "fsdp"), axis=1, tiled=True),
-        lax.all_gather(w_qkv[0], ("dp", "fsdp"), axis=0, tiled=True),
-        lax.all_gather(b_qkv[0], ("dp", "fsdp"), axis=0, tiled=True),
-        lax.all_gather(w_proj[0], ("dp", "fsdp"), axis=0, tiled=True),
-        lax.all_gather(b_proj[0], ("dp", "fsdp"), axis=0, tiled=True),
-        lax.all_gather(w_fc1[0], ("dp", "fsdp"), axis=0, tiled=True),
-        lax.all_gather(b_fc1[0], ("dp", "fsdp"), axis=0, tiled=True),
-        lax.all_gather(w_fc2[0], ("dp", "fsdp"), axis=0, tiled=True),
-        lax.all_gather(b_fc2[0], ("dp", "fsdp"), axis=0, tiled=True),
-        lax.all_gather(layer_scale[0], ("dp", "fsdp"), axis=1, tiled=True),
-    )
-    pos_table = gathered[0].astype(jnp.float32)
-    enc_weights = unpack(gathered[1:])
+    if kernels:
+        line = devices // 8
+        extra = pack(pos_embed, ln_gain, ln_bias, layer_scale, b_proj, b_fc2, b_qkv, b_fc1)
+        wide = gather_all(
+            [extra] + [array[block] for block in (0, 1) for array in (w_qkv, w_proj, w_fc1, w_fc2)],
+            line,
+        )
+        wide = [array.reshape(-1, array.shape[-1]) for array in wide]
+        fold = (b_qkv.shape[1] // pos_embed.shape[1], b_fc1.shape[1] // pos_embed.shape[1])
+        pos, gains, shifts, scales, proj_b, fc2_b, qkv_b, fc1_b = unpack_rows(
+            wide[0], PATCHES, devices, fold
+        )
+        blocks = []
+        for block in (0, 1):
+            qkv, proj, fc1, fc2 = wide[1 + 4 * block : 5 + 4 * block]
+            blocks.append(
+                unpack(
+                    (
+                        gains[block],
+                        shifts[block],
+                        qkv,
+                        qkv_b[block],
+                        proj,
+                        proj_b[block],
+                        fc1,
+                        fc1_b[block],
+                        fc2,
+                        fc2_b[block],
+                        scales[block],
+                    )
+                )
+            )
+        pos_table = pos.astype(jnp.float32)
+        enc_weights, reg_weights = blocks
+    else:
+        pos_table = lax.all_gather(pos_embed, ("dp", "fsdp"), axis=1, tiled=True).astype(jnp.float32)
+        enc_weights, reg_weights = fetch(0, arrays), fetch(1, arrays)
     start = patches.astype(jnp.float32) + jnp.dot(pick_visible, pos_table, precision=highest)
     enc_out, enc_normed, enc_inverse = norm_forward(start, enc_weights[0][0], enc_weights[1][0])
     enc_attn_in = enc_out.astype(jnp.bfloat16)
@@ -259,7 +644,6 @@
     enc_middle = start + enc_weights[10][0] * enc_branch
     enc_feed, enc_feed_kept = feed_forward(enc_middle, enc_weights)
     latent_f = enc_middle + enc_weights[10][1] * enc_feed
-    reg_weights = fetch(1, arrays)
     query_start = jnp.dot(pick_masked, pos_table, precision=highest)
     query_out, query_normed, query_inverse = norm_forward(
         query_start, reg_weights[0][0], reg_weights[1][0]
@@ -280,7 +664,7 @@
     reg_middle = query_start + reg_weights[10][0] * reg_branch
     reg_feed, reg_feed_kept = feed_forward(reg_middle, reg_weights)
     regressed_f = reg_middle + reg_weights[10][1] * reg_feed
-    reg_back = fetch(1, arrays)
+    reg_back = reg_weights
     grad_final = grad_out * live_rows
     reg_scale_late = jnp.sum(grad_final * reg_feed, axis=0)
     grad_from_feed, reg_gain_late, reg_shift_late, reg_feed_grads = feed_backward(
@@ -310,20 +694,7 @@
         + reg_feed_grads
         + (jnp.stack([reg_scale_early, reg_scale_late]),)
     )
-    reg_shards = (
-        lax.psum_scatter(reg_grads[0], ("dp", "fsdp"), scatter_dimension=1, tiled=True),
-        lax.psum_scatter(reg_grads[1], ("dp", "fsdp"), scatter_dimension=1, tiled=True),
-        lax.psum_scatter(reg_grads[2], ("dp", "fsdp"), scatter_dimension=0, tiled=True),
-        lax.psum_scatter(reg_grads[3], ("dp", "fsdp"), scatter_dimension=0, tiled=True),
-        lax.psum_scatter(reg_grads[4], ("dp", "fsdp"), scatter_dimension=0, tiled=True),
-        lax.psum_scatter(reg_grads[5], ("dp", "fsdp"), scatter_dimension=0, tiled=True),
-        lax.psum_scatter(reg_grads[6], ("dp", "fsdp"), scatter_dimension=0, tiled=True),
-        lax.psum_scatter(reg_grads[7], ("dp", "fsdp"), scatter_dimension=0, tiled=True),
-        lax.psum_scatter(reg_grads[8], ("dp", "fsdp"), scatter_dimension=0, tiled=True),
-        lax.psum_scatter(reg_grads[9], ("dp", "fsdp"), scatter_dimension=0, tiled=True),
-        lax.psum_scatter(reg_grads[10], ("dp", "fsdp"), scatter_dimension=1, tiled=True),
-    )
-    enc_back = fetch(0, arrays)
+    enc_back = enc_weights
     grad_finish = grad_latent * live_rows + back_latent
     enc_scale_late = jnp.sum(grad_finish * enc_feed, axis=0)
     grad_from_feed, enc_gain_late, enc_shift_late, enc_feed_grads = feed_backward(
@@ -347,24 +718,55 @@
         + enc_feed_grads
         + (jnp.stack([enc_scale_early, enc_scale_late]),)
     )
-    enc_shards = (
-        lax.psum_scatter(grad_table, ("dp", "fsdp"), scatter_dimension=1, tiled=True),
-        lax.psum_scatter(enc_grads[0], ("dp", "fsdp"), scatter_dimension=1, tiled=True),
-        lax.psum_scatter(enc_grads[1], ("dp", "fsdp"), scatter_dimension=1, tiled=True),
-        lax.psum_scatter(enc_grads[2], ("dp", "fsdp"), scatter_dimension=0, tiled=True),
-        lax.psum_scatter(enc_grads[3], ("dp", "fsdp"), scatter_dimension=0, tiled=True),
-        lax.psum_scatter(enc_grads[4], ("dp", "fsdp"), scatter_dimension=0, tiled=True),
-        lax.psum_scatter(enc_grads[5], ("dp", "fsdp"), scatter_dimension=0, tiled=True),
-        lax.psum_scatter(enc_grads[6], ("dp", "fsdp"), scatter_dimension=0, tiled=True),
-        lax.psum_scatter(enc_grads[7], ("dp", "fsdp"), scatter_dimension=0, tiled=True),
-        lax.psum_scatter(enc_grads[8], ("dp", "fsdp"), scatter_dimension=0, tiled=True),
-        lax.psum_scatter(enc_grads[9], ("dp", "fsdp"), scatter_dimension=0, tiled=True),
-        lax.psum_scatter(enc_grads[10], ("dp", "fsdp"), scatter_dimension=1, tiled=True),
-    )
-    pos_shard = enc_shards[0]
-    weight_shards = tuple(
-        (jnp.stack([early, late]) for early, late in zip(enc_shards[1:], reg_shards))
-    )
+    if kernels:
+        both = [
+            jnp.stack([enc_grads[k], reg_grads[k]]) for k in (0, 1, 10, 5, 9, 3, 7)
+        ]
+        extra = repack(grad_table, *both, devices)
+        order_of = [2, 4, 6, 8]
+        shards = reduce_all(
+            [reg_grads[k].astype(LOW) for k in order_of]
+            + [enc_grads[k].astype(LOW) for k in order_of]
+            + [extra],
+            line,
+        )
+        pos_shard, gains, shifts, scales, proj_b, fc2_b, qkv_b, fc1_b = unpack_rows(
+            shards[8], PATCHES, 1, fold
+        )
+        qkv, proj, fc1, fc2 = [jnp.stack([shards[4 + k], shards[k]]) for k in range(4)]
+        weight_shards = (gains, shifts, qkv, qkv_b, proj, proj_b, fc1, fc1_b, fc2, fc2_b, scales)
+    else:
+        reg_shards = (
+            lax.psum_scatter(reg_grads[0], ("dp", "fsdp"), scatter_dimension=1, tiled=True),
+            lax.psum_scatter(reg_grads[1], ("dp", "fsdp"), scatter_dimension=1, tiled=True),
+            lax.psum_scatter(reg_grads[2], ("dp", "fsdp"), scatter_dimension=0, tiled=True),
+            lax.psum_scatter(reg_grads[3], ("dp", "fsdp"), scatter_dimension=0, tiled=True),
+            lax.psum_scatter(reg_grads[4], ("dp", "fsdp"), scatter_dimension=0, tiled=True),
+            lax.psum_scatter(reg_grads[5], ("dp", "fsdp"), scatter_dimension=0, tiled=True),
+            lax.psum_scatter(reg_grads[6], ("dp", "fsdp"), scatter_dimension=0, tiled=True),
+            lax.psum_scatter(reg_grads[7], ("dp", "fsdp"), scatter_dimension=0, tiled=True),
+            lax.psum_scatter(reg_grads[8], ("dp", "fsdp"), scatter_dimension=0, tiled=True),
+            lax.psum_scatter(reg_grads[9], ("dp", "fsdp"), scatter_dimension=0, tiled=True),
+            lax.psum_scatter(reg_grads[10], ("dp", "fsdp"), scatter_dimension=1, tiled=True),
+        )
+        enc_shards = (
+            lax.psum_scatter(grad_table, ("dp", "fsdp"), scatter_dimension=1, tiled=True),
+            lax.psum_scatter(enc_grads[0], ("dp", "fsdp"), scatter_dimension=1, tiled=True),
+            lax.psum_scatter(enc_grads[1], ("dp", "fsdp"), scatter_dimension=1, tiled=True),
+            lax.psum_scatter(enc_grads[2], ("dp", "fsdp"), scatter_dimension=0, tiled=True),
+            lax.psum_scatter(enc_grads[3], ("dp", "fsdp"), scatter_dimension=0, tiled=True),
+            lax.psum_scatter(enc_grads[4], ("dp", "fsdp"), scatter_dimension=0, tiled=True),
+            lax.psum_scatter(enc_grads[5], ("dp", "fsdp"), scatter_dimension=0, tiled=True),
+            lax.psum_scatter(enc_grads[6], ("dp", "fsdp"), scatter_dimension=0, tiled=True),
+            lax.psum_scatter(enc_grads[7], ("dp", "fsdp"), scatter_dimension=0, tiled=True),
+            lax.psum_scatter(enc_grads[8], ("dp", "fsdp"), scatter_dimension=0, tiled=True),
+            lax.psum_scatter(enc_grads[9], ("dp", "fsdp"), scatter_dimension=0, tiled=True),
+            lax.psum_scatter(enc_grads[10], ("dp", "fsdp"), scatter_dimension=1, tiled=True),
+        )
+        pos_shard = enc_shards[0]
+        weight_shards = tuple(
+            (jnp.stack([early, late]) for early, late in zip(enc_shards[1:], reg_shards))
+        )
     return (
         latent_f.astype(jnp.bfloat16),
         regressed_f.astype(jnp.bfloat16),
@@ -409,4 +811,18 @@
         P(None, ("dp", "fsdp")),
         P(None, None, ("dp", "fsdp")),
     )
-    return jax.shard_map(local, mesh=mesh, in_specs=in_specs, out_specs=out_specs, check_vma=False)
+    devices = mesh.shape["dp"] * mesh.shape["fsdp"]
+
+    def step(*args):
+        rows = args[7].shape[1]
+        kernels = mesh.shape["fsdp"] == 4 and rows // (devices // 2) % 16 == 0
+        run = jax.shard_map(
+            functools.partial(local, kernels, devices),
+            mesh=mesh,
+            in_specs=in_specs,
+            out_specs=out_specs,
+            check_vma=False,
+        )
+        return run(*args)
+
+    return step

time: 1880 us -> 611 us (0.33)
  waiting for transfers between devices: 1190 us -> 0 us
  blocking collectives: 318 us -> 0 us
  Pallas kernels: 0 us -> 287 us
    reduce_scatter x9 -> x0, waiting for transfers between devices: 1100 us -> none  [the longest x1 141 us: local(): lax.psum_scatter(enc_grads[8], ('dp', 'fsdp'), scatter_dimension=0, tiled...]
    pallas_call x0 -> x2, Pallas kernels: none -> 287 us  [the longest x1 147 us: reduce_all(): pl.pallas_call(functools.partial(reduce_body, line, items), out_shape=[ja...]
    all_gather x7 -> x0, blocking collectives: 276 us -> none  [the longest x1 41.7 us: local(): lax.all_gather(ln_gain[0], ('dp', 'fsdp'), axis=1, tiled=True)]
    unnamed x19 -> x0, waiting for transfers between devices: 61.3 us -> none
    unnamed x1 -> x0, blocking collectives: 42.3 us -> none
    all_gather x8 -> x0, waiting for transfers between devices: 28.9 us -> none  [the longest x1 28.8 us: fetch(): lax.all_gather(w_fc2[block], ('dp', 'fsdp'), axis=0, tiled=True)]
  transfers between devices with their start and end apart: 18 -> 0, of which waited for: 11 -> 0; matrix products, arithmetic and copies ran while one was open for 13% -> 0% of each run, Pallas kernels for 0% -> 0%
where the time goes in v1:
time: 611 us; the launch traced here: 601 us
  Pallas kernels  287 us (47%)
  matrix products  173 us (28%)
  local copies, waits for them, and re-layouts  95.7 us (16%)
  other arithmetic  41.3 us (7%)
    pallas_call x1, Pallas kernels, reduce_all(): pl.pallas_call(functools.partial(reduce_body, line, items), out_shape=[ja...  147 us
    pallas_call x1, Pallas kernels, gather_all(): pl.pallas_call(functools.partial(gather_body, line, items), out_shape=[ja...  140 us
    dot_general x10, matrix products, outer_rows(): jnp.einsum('rd,rf->df', left, right, preferred_element_type=jnp.float32)  39.5 us
    unnamed x347, local copies, waits for them, and re-layouts  33.4 us
    dot_general x2, matrix products, feed_forward(): branch = jnp.dot(active, w_fc2, preferred_element_type=jnp.float32) + b_fc2  18.1 us
    dot_general x2, matrix products, feed_backward(): grad_active = jnp.dot(grad_low, w_fc2.T, preferred_element_type=jnp.float32)  17.8 us
    dot_general x2, matrix products, feed_backward(): jnp.dot(grad_hidden, w_fc1.T, preferred_element_type=jnp.float32)  13.1 us

profile of v1, /device:TPU:0, one launch (start us, length us, event | category | flops | bytes accessed | tf_op | source)
XLA Modules:
  0.0 600.7 jit_solution(5720238398886158316)
XLA Ops:
  4.9 139.9 %gather_all.1 = (bf16[4,4,48,256]{3,2,1,0:T(8,128)(2,1)S(1)}, bf16[4,4,48,2304]{3,2,1,0:T(8,128)(2,1)S(1)}, bf16[4,4,48,768]{3,2,1,0:T(8,128)(2,1)S(1)}, bf16[4,...) custom-call(bf16[24,256]{1,0:T(8,128)(2,1)S(1)} %pad.16.refs_0_, ...), custom_call_target="tpu_custom_call" | custom-call | tf_op jit(solution)/shard_map/gather_all/pallas_call | solution.py:166
  147.3 2.2 copy-done.3
  149.5 2.2 copy-done.4
  153.8 2.2 copy-done.6
  167.2 2.9 add_convert_fusion.6
  172.6 3.3 fusion.30
  181.1 2.2 fusion.154
  185.1 2.4 fusion.37
  190.0 2.9 fusion.65
  196.9 4.9 fusion.134
  203.0 9.9 %fusion.147 = (f32[512]{0:T(512)S(1)}, f32[512,768]{1,0:T(8,128)S(1)}, f32[512,768]{1,0:T(8,128)}) fusion(f32[512,768]{1,0:T(8,128)} %copy-done.24, f32[768]{0:T(1024)S(1)} %get-tuple-element.118, f32[768]{0:T(1024)S(1)} %copy-done.114, bf16[3072,768]{1,0:T(8,128)(2,1)} %bitcast.283, f32[512,3072]{1,0:T(8,128)} %fusion.134, f32[3072]{0:T(1024)S(1)} %reshape.486), kind=kOutput, calls=%fused_computation.314 | convolution fusion | flops 2433220096 | bytes 15749120 | tf_op jit(solution)/shard_map/dot_general | solution.py:487
  215.5 2.1 copy-done.1
  217.6 4.6 fusion.26
  222.4 3.2 fusion.18
  225.6 2.6 copy.155
  228.2 3.9 reshape.458
  232.2 2.9 add_convert_fusion.2
  235.2 2.3 copy.157
  239.2 3.3 slice.427
  242.5 2.6 copy.158
  245.1 3.9 reshape.460
  249.0 3.2 fusion.156
  252.2 2.3 fusion.14
  255.3 3.2 fusion.62
  262.4 4.8 fusion.135
  269.2 9.8 %fusion.140 = (bf16[3072]{0:T(1024)(128)(2,1)}, bf16[512,3072]{1,0:T(8,128)(2,1)S(1)}) fusion(f32[512,3072]{1,0:T(8,128)} %fusion.135, f32[3072]{0:T(1024)S(1)} %reshape.489, bf16[512,768]{1,0:T(8,128)(2,1)} %get-tuple-element.140, bf16[3072,768]{1,0:T(8,128)(2,1)} %bitcast.287), kind=kOutput, calls=%fused_computation.308 | convolution fusion | flops 2450519040 | bytes 14960640 | tf_op jit(solution)/shard_map/dot_general | solution.py:497
  279.0 6.2 %fusion.161 = f32[512,768]{1,0:T(8,128)S(1)} fusion(bf16[512,3072]{1,0:T(8,128)(2,1)S(1)} %get-tuple-element.135, bf16[768,3072]{1,0:T(8,128)(2,1)} %bitcast.289), kind=kOutput, calls=%fused_computation.328 | convolution fusion | flops 2415919104 | bytes 9437184 | tf_op jit(solution)/shard_map/dot_general | solution.py:502
  285.3 8.3 %multiply_reduce_fusion.2 = (bf16[768]{0:T(1024)(128)(2,1)}, bf16[512,768]{1,0:T(8,128)(2,1)}, bf16[768]{0:T(1024)(128)(2,1)}, f32[512]{0:T(512)S(1)}, f32[512]{0:T(512)S(1)}, /*index=5*/bf16[768]{0:T(1024)(128)(2,1)}) fusion(f32[512,768]{1,0:T(8,128)S(1)} %copy-done.36, f32[512]{0:T(512)S(1)} %copy-done.94, f32[768]{0:T(1024)S(1)} %copy-done.138, ...), kind=kOutput, calls=%fused_computation.71 | convolution fusion | flops 2437935872 | bytes 16551424 | tf_op jit(solution)/shard_map/dot_general | solution.py:487
  293.6 2.5 fusion.145
  298.8 2.3 copy.164
  302.9 4.8 multiply_reduce_fusion
  308.0 2.2 multiply_convert_fusion
  317.4 4.1 fusion.157
  324.7 5.1 fusion.24
  331.4 5.1 multiply_reduce_fusion.7
  338.6 8.0 %fusion.138 = (bf16[3072]{0:T(1024)(128)(2,1)S(1)}, bf16[512,3072]{1,0:T(8,128)(2,1)}) fusion(f32[512,3072]{1,0:T(8,128)S(1)} %bitcast.370, f32[3072]{0:T(1024)S(1)} %copy-done.123, bf16[512,768]{1,0:T(8,128)(2,1)S(1)} %get-tuple-element.137, bf16[3072,768]{1,0:T(8,128)(2,1)S(1)} %bitcast.286), kind=kOutput, calls=%fused_computation.307 | convolution fusion | flops 2450519040 | bytes 14960640 | tf_op jit(solution)/shard_map/dot_general | solution.py:497
  347.1 6.9 %multiply_reduce_fusion.8 = (bf16[768]{0:T(1024)(128)(2,1)S(1)}, f32[512]{0:T(512)S(1)}, f32[512]{0:T(512)S(1)}, bf16[768]{0:T(1024)(128)(2,1)S(1)}, f32[512,768]{1,0:T(8,128)S(1)}) fusion(f32[512,768]{1,0:T(8,128)} %copy-done.24, f32[512]{0:T(512)S(1)} %copy-done.132, f32[512]{0:T(512)S(1)} %copy-done.107, f32[768]{0:T(1024)S(1)} %copy-done.109, ...), kind=kOutput, calls=%fused_computation.77 | convolution fusion | flops 2419455488 | bytes 11024384 | tf_op jit(solution)/shard_map/dot_general | solution.py:502
  360.0 3.4 multiply_reduce_fusion.1
  366.2 4.2 fusion.159
  371.2 2.2 multiply_reduce_fusion.4
  385.7 3.5 fusion.39
  391.6 8.7 %convolution_convert_fusion = bf16[3072,768]{1,0:T(8,128)(2,1)} fusion(bf16[512,768]{1,0:T(8,128)(2,1)S(1)} %copy-done.58, f32[512,3072]{1,0:T(8,128)} %fusion.134, f32[3072]{0:T(1024)S(1)} %copy-done.123), kind=kOutput, calls=%fused_computation.27 | convolution fusion | flops 2434007040 | bytes 11808768 | tf_op jit(solution)/shard_map/rd,rf->df/dot_general | solution.py:385
  400.4 5.0 convolution_convert_fusion.1
  411.5 2.1 pad_maximum_fusion.1.refs_4_
  415.1 4.8 convolution_convert_fusion.3
  426.6 4.6 convolution_convert_fusion.4
  433.2 8.7 %convolution_convert_fusion.2 = bf16[3072,768]{1,0:T(8,128)(2,1)} fusion(bf16[512,768]{1,0:T(8,128)(2,1)S(1)} %copy-done.63, f32[512,3072]{1,0:T(8,128)} %fusion.135, f32[3072]{0:T(1024)S(1)} %copy-done.125), kind=kOutput, calls=%fused_computation.29 | convolution fusion | flops 2434007040 | bytes 11808768 | tf_op jit(solution)/shard_map/rd,rf->df/dot_general | solution.py:385
  442.0 147.4 %reduce_all.1 = (f32[24,2304]{1,0:T(8,128)}, f32[24,768]{1,0:T(8,128)}, f32[24,3072]{1,0:T(8,128)}, f32[96,768]{1,0:T(8,128)}, f32[24,2304]{1,0:T(8,128)}, /*ind...) custom-call(bf16[4,4,48,2304]{3,2,1,0:T(8,128)(2,1)} %pad_maximum_fusion.refs_0_, ...), custom_call_target="tpu_custom_call" | custom-call | tf_op jit(solution)/shard_map/reduce_all/pallas_call | solution.py:314
  (540 shorter events, 117.2 us)
Async XLA Ops:
  1.8 157.7 %copy-start.139 = (s32[4,196]{1,0:T(4,128)S(1)}, s32[4,196]{1,0:T(4,128)}, u32[]{:S(2)}) copy-start(s32[4,196]{1,0:T(4,128)} %param.17) | copy-start | bytes 9412
  1.8 157.7 %copy-start.148 = (pred[128]{0:T(512)(128)(4,1)S(1)}, pred[128]{0:T(512)(128)(4,1)}, u32[]{:S(2)}) copy-start(pred[128]{0:T(512)(128)(4,1)} %constant.40.clone.1) | copy-start | bytes 388
  194.1 8.8 %copy-start.112 = (f32[768]{0:T(1024)}, f32[768]{0:T(1024)S(1)}, u32[]{:S(2)}) copy-start(f32[768]{0:T(1024)S(1)} %get-tuple-element.118) | copy-start | bytes 9220
  196.2 5.6 copy-start.24
  196.2 5.6 copy-start.106
  196.6 5.3 copy-start.131
  196.9 6.1 %copy-start.114 = (f32[768]{0:T(1024)S(1)}, f32[768]{0:T(1024)}, u32[]{:S(2)}) copy-start(f32[768]{0:T(1024)} %get-tuple-element.230) | copy-start | bytes 9220
  203.0 9.9 %copy-start.122 = (f32[3072]{0:T(1024)}, f32[3072]{0:T(1024)S(1)}, u32[]{:S(2)}) copy-start(f32[3072]{0:T(1024)S(1)} %reshape.486) | copy-start | bytes 36868
  214.6 47.7 %copy-start.136 = (f32[768]{0:T(1024)}, f32[768]{0:T(1024)S(1)}, u32[]{:S(2)}) copy-start(f32[768]{0:T(1024)S(1)} %get-tuple-element.124) | copy-start | bytes 9220
  214.6 79.0 %copy-start.110 = (f32[768]{0:T(1024)}, f32[768]{0:T(1024)S(1)}, u32[]{:S(2)}) copy-start(f32[768]{0:T(1024)S(1)} %get-tuple-element.226) | copy-start | bytes 9220
  215.3 16.9 %copy-start.29 = (bf16[512,768]{1,0:T(8,128)(2,1)}, bf16[512,768]{1,0:T(8,128)(2,1)S(1)}, u32[]{:S(2)}) copy-start(bf16[512,768]{1,0:T(8,128)(2,1)S(1)} %get-tuple-element.193) | copy-start | bytes 2359300
  215.5 6.8 %copy-start.32 = (bf16[4,256,768]{2,1,0:T(8,128)(2,1)}, bf16[4,256,768]{2,1,0:T(8,128)(2,1)S(1)}, u32[]{:S(2)}) copy-start(bf16[4,256,768]{2,1,0:T(8,128)(2,1)S(1)} %pad_maximum_fusion.5) | copy-start | bytes 4718596
  252.2 10.2 %slice-start.4 = ((s8[4718592]{0:T(1024)(128)(4,1)}), s8[4194304]{0:T(1024)(128)(4,1)S(1)}, s32[]{:S(2)}) async-start(s8[4718592]{0:T(1024)(128)(4,1)} %bitcast.290), calls=%async_computation.4 | async-start | bytes 8388608
  255.3 7.0 %slice-start.5 = ((s8[4718592]{0:T(1024)(128)(4,1)}), s8[524288]{0:T(1024)(128)(4,1)S(1)}, s32[]{:S(2)}) async-start(s8[4718592]{0:T(1024)(128)(4,1)} %bitcast.290), calls=%async_computation.5 | async-start | bytes 1048576
  262.0 5.2 copy-start.20
  262.0 31.6 %copy-start.100 = (f32[512]{0:T(512)}, f32[512]{0:T(512)S(1)}, u32[]{:S(2)}) copy-start(f32[512]{0:T(512)S(1)} %broadcast_multiply_fusion.9) | copy-start | bytes 6148
  262.3 31.3 %copy-start.127 = (f32[512]{0:T(512)}, f32[512]{0:T(512)S(1)}, u32[]{:S(2)}) copy-start(f32[512]{0:T(512)S(1)} %add_rsqrt_fusion) | copy-start | bytes 6148
  269.2 16.1 %copy-start.124 = (f32[3072]{0:T(1024)}, f32[3072]{0:T(1024)S(1)}, u32[]{:S(2)}) copy-start(f32[3072]{0:T(1024)S(1)} %reshape.489) | copy-start | bytes 36868
  279.0 6.2 %copy-start.156 = (bf16[512,3072]{1,0:T(8,128)(2,1)}, bf16[512,3072]{1,0:T(8,128)(2,1)S(1)}, u32[]{:S(2)}) copy-start(bf16[512,3072]{1,0:T(8,128)(2,1)S(1)} %get-tuple-element.135) | copy-start | bytes 9437188
  279.0 6.2 %copy-start.21 = (f32[512,768]{1,0:T(8,128)S(1)}, f32[512,768]{1,0:T(8,128)}, u32[]{:S(2)}) copy-start(f32[512,768]{1,0:T(8,128)} %copy-done.20) | copy-start | bytes 4718596
  279.0 6.3 %copy-start.36 = (f32[512,768]{1,0:T(8,128)S(1)}, f32[512,768]{1,0:T(8,128)}, u32[]{:S(2)}) copy-start(f32[512,768]{1,0:T(8,128)} %param.19) | copy-start | bytes 4718596
  279.0 6.3 %copy-start.138 = (f32[768]{0:T(1024)S(1)}, f32[768]{0:T(1024)}, u32[]{:S(2)}) copy-start(f32[768]{0:T(1024)} %get-tuple-element.116) | copy-start | bytes 9220
  279.0 6.3 %copy-start.155 = (f32[512,3072]{1,0:T(8,128)S(1)}, f32[512,3072]{1,0:T(8,128)}, u32[]{:S(2)}) copy-start(f32[512,3072]{1,0:T(8,128)} %fusion.135) | copy-start | bytes 18874372
  302.9 5.2 slice-start.7
  324.7 5.6 copy-start.19
  324.7 5.6 copy-start.45
  329.9 8.5 %slice-start.2 = ((s8[4718592]{0:T(1024)(128)(4,1)}), s8[4194304]{0:T(1024)(128)(4,1)S(1)}, s32[]{:S(2)}) async-start(s8[4718592]{0:T(1024)(128)(4,1)} %bitcast.284), calls=%async_computation.2 | async-start | bytes 8388608
  329.9 8.5 %slice-start.8 = ((s8[6291456]{0:T(1024)(128)(4,1)}), s8[2097152]{0:T(1024)(128)(4,1)S(1)}, s32[]{:S(2)}) async-start(s8[6291456]{0:T(1024)(128)(4,1)} %bitcast.369), calls=%async_computation.8 | async-start | bytes 4194304
  331.3 5.2 copy-start.53
  331.3 5.2 copy-start.95
  331.3 5.2 copy-start.115
  331.3 7.1 %slice-start.3 = ((s8[4718592]{0:T(1024)(128)(4,1)}), s8[524288]{0:T(1024)(128)(4,1)S(1)}, s32[]{:S(2)}) async-start(s8[4718592]{0:T(1024)(128)(4,1)} %bitcast.284), calls=%async_computation.3 | async-start | bytes 1048576
  331.3 7.1 %slice-start.9 = ((s8[6291456]{0:T(1024)(128)(4,1)}), s8[4194304]{0:T(1024)(128)(4,1)S(1)}, s32[]{:S(2)}) async-start(s8[6291456]{0:T(1024)(128)(4,1)} %bitcast.369), calls=%async_computation.9 | async-start | bytes 8388608
  338.5 8.1 %copy-start.57 = (bf16[512,768]{1,0:T(8,128)(2,1)}, bf16[512,768]{1,0:T(8,128)(2,1)S(1)}, u32[]{:S(2)}) copy-start(bf16[512,768]{1,0:T(8,128)(2,1)S(1)} %get-tuple-element.137) | copy-start | bytes 2359300
  338.5 8.2 %copy-start.133 = (bf16[3072]{0:T(1024)(128)(2,1)S(1)}, bf16[3072]{0:T(1024)(128)(2,1)}, u32[]{:S(2)}) copy-start(bf16[3072]{0:T(1024)(128)(2,1)} %get-tuple-element.134) | copy-start | bytes 18436
  338.5 8.5 %copy-start.107 = (f32[512]{0:T(512)S(1)}, f32[512]{0:T(512)}, u32[]{:S(2)}) copy-start(f32[512]{0:T(512)} %copy-done.106) | copy-start | bytes 6148
  338.5 8.5 %copy-start.109 = (f32[768]{0:T(1024)S(1)}, f32[768]{0:T(1024)}, u32[]{:S(2)}) copy-start(f32[768]{0:T(1024)} %get-tuple-element.128) | copy-start | bytes 9220
  338.6 8.5 %copy-start.132 = (f32[512]{0:T(512)S(1)}, f32[512]{0:T(512)}, u32[]{:S(2)}) copy-start(f32[512]{0:T(512)} %copy-done.131) | copy-start | bytes 6148
  347.0 6.9 %copy-start.25 = (f32[512,768]{1,0:T(8,128)S(1)}, f32[512,768]{1,0:T(8,128)}, u32[]{:S(2)}) copy-start(f32[512,768]{1,0:T(8,128)} %copy-done.24) | copy-start | bytes 4718596
  347.1 6.9 %copy-start.28 = (f32[512,768]{1,0:T(8,128)S(1)}, f32[512,768]{1,0:T(8,128)}, u32[]{:S(2)}) copy-start(f32[512,768]{1,0:T(8,128)} %get-tuple-element.138) | copy-start | bytes 4718596
  366.2 5.0 copy-start.113
  374.0 6.0 copy-start.59
  391.6 8.7 %copy-start.26 = (f32[512,768]{1,0:T(8,128)S(1)}, f32[512,768]{1,0:T(8,128)}, u32[]{:S(2)}) copy-start(f32[512,768]{1,0:T(8,128)} %copy-done.24) | copy-start | bytes 4718596
  391.6 8.7 %copy-start.135 = (f32[768]{0:T(1024)S(1)}, f32[768]{0:T(1024)}, u32[]{:S(2)}) copy-start(f32[768]{0:T(1024)} %get-tuple-element.228) | copy-start | bytes 9220
  391.6 8.7 %copy-start.158 = (bf16[512,3072]{1,0:T(8,128)(2,1)S(1)}, bf16[512,3072]{1,0:T(8,128)(2,1)}, u32[]{:S(2)}) copy-start(bf16[512,3072]{1,0:T(8,128)(2,1)} %get-tuple-element.133) | copy-start | bytes 9437188
  400.3 5.0 copy-start.42
  400.3 5.0 copy-start.65
  589.4 5.4 copy-start.67
  (121 other events, 284.5 us)
